TPU v7x, 512 devices: a whole 4x4x16 slice. The times are simulated.
512 devices in a mesh: brow: 16 (over y, x), bcol: 32 (over z, core).
Axes of the slice: x: 4, y: 4, z: 16, core: 2. Of those that a mesh axis runs over, the one named last changes fastest.
Arguments:
- gradient: bfloat16 [8192, 8192], P(('brow', 'bcol')), may hold values from -1.5 to 1.5
- left_stats: float32 [16, 8192, 512], P('brow', 'bcol'), may hold values from -1 to 8, as said below
- right_stats: float32 [16, 8192, 512], P('brow', 'bcol'), may hold values from -1 to 8, as said below
- left_roots: bfloat16 [16, 8192, 512], P('brow', 'bcol'), may hold values from -1 to 3, as said below
- right_roots: bfloat16 [16, 8192, 512], P('brow', 'bcol'), may hold values from -1 to 3, as said below
- refresh: int32 [16, 4], P('brow'), may hold values from 0 to 15, as said below
Outputs:
- update: bfloat16 [8192, 8192], P(('brow', 'bcol'))
- new_left_stats: float32 [16, 8192, 512], P('brow', 'bcol')
- new_right_stats: float32 [16, 8192, 512], P('brow', 'bcol')
- new_left_roots: bfloat16 [16, 8192, 512], P('brow', 'bcol')
- new_right_roots: bfloat16 [16, 8192, 512], P('brow', 'bcol')
Inputs may be any that keep to these rules, and one draw needn't show every extreme that they name: `refresh`: each row names 4 different block columns; some block row lists column 15 and another block row lists column 0. `left_stats`: every 512 x 512 block is symmetric positive definite. `right_stats`: every 512 x 512 block is symmetric positive definite. `left_roots`: every 512 x 512 block is symmetric. `right_roots`: every 512 x 512 block is symmetric.
All inputs are finite; a program needn't handle non-finite values.
Results may differ from a plain program's by a relative error of at most 0.005.
Values may be sent and summed in bfloat16 or wider, within the bound.
A program may use at most 64 MiB of HBM per device.

v0:
```python
import jax
import jax.numpy as jnp
from jax import lax
from jax.sharding import PartitionSpec as P

ITERS = 3


decay = 0.9
epsilon = 1e-06
highest = lax.Precision.HIGHEST


def from_partner(shard, axis, stride):
    return lax.ppermute(shard, axis, [(i, i ^ 1 << stride) for i in range(lax.axis_size(axis))])


def product(left_side, right_side):
    return jnp.dot(left_side, right_side, precision=highest)


def unchanged(matrix):
    return matrix


def inverse_rows(row_block, collect):
    row_count, order_size = row_block.shape
    eye_rows = (
        lax.broadcasted_iota(jnp.int32, (row_count, order_size), 0)
        == lax.broadcasted_iota(jnp.int32, (row_count, order_size), 1)
    ).astype(jnp.float32)
    eye_full = jnp.eye(order_size, dtype=jnp.float32)
    shifted = row_block + epsilon * eye_rows
    whole_matrix = collect(shifted)
    scaling = 2.5 / jnp.sqrt(jnp.sum(whole_matrix * whole_matrix))
    moment_full = scaling * whole_matrix
    iterate = jnp.sqrt(jnp.sqrt(scaling)) * eye_rows
    for iteration in range(ITERS):
        factor = (5.0 * eye_full - moment_full) * 0.25
        square = product(factor, factor)
        fourth_rows = product(square, square)
        moment_rows = product(fourth_rows, moment_full)
        iterate = product(iterate, factor)
        if iteration + 1 < ITERS:
            moment_full = collect(moment_rows)
    return iterate.astype(jnp.bfloat16)


def body(gradient, left_stats, right_stats, left_roots, right_roots, refresh):
    position = lax.axis_index("bcol")
    half = position % 2
    block_col = position // 2
    order_size = left_stats.shape[2]
    half_rows = order_size // 2
    is_second = half == 1
    mine = lax.all_to_all(gradient, "bcol", split_axis=1, concat_axis=0, tiled=True)
    left_root_mine = left_roots[0]
    partner_grad, partner_left = from_partner((mine, left_root_mine), "bcol", 0)
    grad_full = jnp.where(
        is_second,
        jnp.concatenate([partner_grad, mine], 1),
        jnp.concatenate([mine, partner_grad], 1),
    )
    left_root_full = jnp.where(
        is_second,
        jnp.concatenate([partner_left, left_root_mine], 0),
        jnp.concatenate([left_root_mine, partner_left], 0),
    )
    grad_rows = lax.dynamic_slice_in_dim(grad_full, half * half_rows, half_rows, 0)
    left_gram = lax.dot_general(
        grad_rows, grad_full, (((1,), (1,)), ((), ())), preferred_element_type=jnp.float32
    )
    right_gram = lax.dot_general(
        mine, grad_full, (((0,), (0,)), ((), ())), preferred_element_type=jnp.float32
    )
    left_new = decay * left_stats[0] + (1.0 - decay) * left_gram
    right_new = decay * right_stats[0] + (1.0 - decay) * right_gram
    right_part = lax.dot_general(
        grad_full, right_roots[0], (((1,), (1,)), ((), ())), preferred_element_type=jnp.float32
    ).astype(jnp.bfloat16)
    update_cols = jnp.dot(left_root_full, right_part, preferred_element_type=jnp.float32).astype(
        jnp.bfloat16
    )
    update = lax.all_to_all(update_cols, "bcol", split_axis=0, concat_axis=1, tiled=True)
    chosen = refresh[0]
    listed = jnp.any(chosen == block_col)
    mine_side = jnp.where(is_second, right_new, left_new)
    partner_side = from_partner(
        jnp.where(is_second, left_new, right_new).astype(jnp.bfloat16), "bcol", 0
    ).astype(jnp.float32)
    whole_side = jnp.where(
        is_second,
        jnp.concatenate([partner_side, mine_side], 0),
        jnp.concatenate([mine_side, partner_side], 0),
    )
    root_full = inverse_rows(whole_side, unchanged)
    own_rows = lax.dynamic_slice_in_dim(root_full, half * half_rows, half_rows, 0)
    given_rows = lax.dynamic_slice_in_dim(root_full, (1 - half) * half_rows, half_rows, 0)
    taken = from_partner(given_rows, "bcol", 0)
    left_fresh = jnp.where(is_second, taken, own_rows)
    right_fresh = jnp.where(is_second, own_rows, taken)
    left_out = jnp.where(listed, left_fresh, left_roots[0])
    right_out = jnp.where(listed, right_fresh, right_roots[0])
    return (update, left_new[None], right_new[None], left_out[None], right_out[None])


def solution(mesh):
    in_specs = (
        P(("brow", "bcol"), None),
        P("brow", "bcol", None),
        P("brow", "bcol", None),
        P("brow", "bcol", None),
        P("brow", "bcol", None),
        P("brow", None),
    )
    out_specs = (
        P(("brow", "bcol"), None),
        P("brow", "bcol", None),
        P("brow", "bcol", None),
        P("brow", "bcol", None),
        P("brow", "bcol", None),
    )
    return jax.shard_map(body, mesh=mesh, in_specs=in_specs, out_specs=out_specs, check_vma=False)
```

profile of v0, /device:TPU:1, one launch (start us, length us, event | category | flops | bytes accessed | tf_op | source)
XLA Modules:
  0.0 81.7 jit_solution(4765321679728686356)
XLA Ops:
  0.6 1.7 %copy.16 = bf16[2,32,8,256]{3,2,0,1:T(8,128)(2,1)} copy(bf16[2,32,8,256]{3,2,1,0:T(8,128)(2,1)} %bitcast.55) | data formatting | bytes 524288 | tf_op jit(solution)/shard_map/all_to_all | solution.py:56
  2.3 0.0 copy-start.3
  2.3 0.0 copy-start.5
  2.3 16.9 %all-to-all-start = ((bf16[16,32,256]{2,0,1:T(8,128)(2,1)}), bf16[16,32,256]{2,0,1:T(8,128)(2,1)S(1)}, u32[]{:S(2)}, u32[]{:S(2)}) async-start(bf16[16,32,256]{2,0,1:T(8,128)(2,1)} %bitcast.45), calls=%async_computation | async-start | bytes 524288 | tf_op jit(solution)/shard_map/all_to_all | solution.py:56
  19.2 0.0 copy-done.3
  19.2 2.1 %collective-permute-start = (bf16[256,512]{1,0:T(8,128)(2,1)S(1)}, bf16[256,512]{1,0:T(8,128)(2,1)S(1)}, u32[]{:S(2)}, u32[]{:S(2)}) collective-permute-start(bf16[256,512]{1,0:T(8,128)(2,1)S(1)} %bitcast.53), channel_id=1, source_target_pairs={{0,1},{1,0},{2,3},{3,2},{4,5},{5,4},{6,7},{7,6},{8,9},{9,8},{10,11... | collective-permute-start | bytes 786440 | tf_op jit(solution)/shard_map/ppermute | solution.py:15
  21.4 19.8 %all-to-all-done = bf16[16,32,256]{2,0,1:T(8,128)(2,1)S(1)} async-done(((bf16[16,32,256]{2,0,1:T(8,128)(2,1)}), bf16[16,32,256]{2,0,1:T(8,128)(2,1)S(1)}, u32[]{:S(2)}, u32[]{:S(2)}) %all-to-all-start) | async-done | bytes 262176 | tf_op jit(solution)/shard_map/all_to_all | solution.py:56
  41.2 2.9 %collective-permute-start.1 = (bf16[512,256]{1,0:T(8,128)(2,1)S(1)}, bf16[512,256]{1,0:T(8,128)(2,1)S(1)}, u32[]{:S(2)}, u32[]{:S(2)}) collective-permute-start(bf16[512,256]{1,0:T(8,128)(2,1)S(1)} %bitcast.49), channel_id=1, source_target_pairs={{0,1},{1,0},{2,3},{3,2},{4,5},{5,4},{6,7},{7,6},{8,9},{9,8},{10,11... | collective-permute-start | bytes 786440 | tf_op jit(solution)/shard_map/ppermute | solution.py:15
  44.1 0.0 collective-permute-done
  44.1 1.1 %collective-permute-done.1 = bf16[512,256]{1,0:T(8,128)(2,1)S(1)} collective-permute-done((bf16[512,256]{1,0:T(8,128)(2,1)S(1)}, bf16[512,256]{1,0:T(8,128)(2,1)S(1)}, u32[]{:S(2)}, u32[]{:S(2)}) %collective-permute-start.1) | collective-permute-done | bytes 262176 | tf_op jit(solution)/shard_map/ppermute | solution.py:15
  45.2 0.0 copy-done.5
  45.2 1.5 %convolution_convert_fusion.1 = bf16[512,256]{1,0:T(8,128)(2,1)} fusion(bf16[256,512]{1,0:T(8,128)(2,1)S(1)} %bitcast.54, bf16[256,512]{1,0:T(8,128)(2,1)S(1)} %collective-permute-done, pred[]{:T(512)S(6)} %eq.24, bf16[1,256,512]{2,1,0:T(8,128)(2,1)S(1)} %copy-done.5, bf16[512,256]{1,0:T(8,128)(2,1)S(1)} %bitcast.50, ...), kind=kOutput, calls=%fused_computation.10 | convolution fusion | flops 273416192 | bytes 1572865 | tf_op jit(solution)/shard_map/dot_general | solution.py:81
  46.7 3.9 %all-to-all-start.1 = ((bf16[32,16,256]{2,1,0:T(8,128)(2,1)}), bf16[32,16,256]{2,1,0:T(8,128)(2,1)S(1)}, u32[]{:S(2)}, u32[]{:S(2)}) async-start(bf16[32,16,256]{2,1,0:T(8,128)(2,1)} %bitcast.5), calls=%async_computation.1 | async-start | bytes 524288 | tf_op jit(solution)/shard_map/all_to_all | solution.py:84
  50.6 0.0 copy-start.7
  50.6 0.1 maximum_select_fusion.3
  50.8 0.9 %copy-done.7 = f32[1,256,512]{2,1,0:T(8,128)S(1)} copy-done((f32[1,256,512]{2,1,0:T(8,128)S(1)}, f32[1,256,512]{2,1,0:T(8,128)}, u32[]{:S(2)}) %copy-start.7) | copy-done | bytes 524312
  51.7 0.0 copy-start.2
  51.7 0.3 fusion.2
  52.0 0.7 copy-done.2
  52.7 0.0 copy-start
  52.7 0.4 select_convert_fusion
  53.1 0.0 copy-start.1
  53.1 2.4 %collective-permute-start.2 = (bf16[256,512]{1,0:T(8,128)(2,1)S(1)}, bf16[256,512]{1,0:T(8,128)(2,1)S(1)}, u32[]{:S(2)}, u32[]{:S(2)}) collective-permute-start(bf16[256,512]{1,0:T(8,128)(2,1)S(1)} %get-tuple-element.7), channel_id=1, source_target_pairs={{0,1},{1,0},{2,3},{3,2},{4,5},{5,4},{6,7},{7,6},{8,9},{9,8},{10,11... | collective-permute-start | bytes 786440 | tf_op jit(solution)/shard_map/ppermute | solution.py:15
  55.5 0.0 copy-done
  55.5 0.1 broadcast_select_fusion
  55.6 0.0 copy-done.1
  55.6 0.9 %collective-permute-done.2 = bf16[256,512]{1,0:T(8,128)(2,1)S(1)} collective-permute-done((bf16[256,512]{1,0:T(8,128)(2,1)S(1)}, bf16[256,512]{1,0:T(8,128)(2,1)S(1)}, u32[]{:S(2)}, u32[]{:S(2)}) %collective-permute-start.2) | collective-permute-done | bytes 262176 | tf_op jit(solution)/shard_map/ppermute | solution.py:15
  56.6 0.9 %multiply_reduce_fusion = f32[]{:T(128)} fusion(f32[256,512]{1,0:T(8,128)S(1)} %convert_element_type.20, f32[256,512]{1,0:T(8,128)S(1)} %broadcast_select_fusion, pred[]{:T(512)S(6)} %eq.24), kind=kLoop, calls=%fused_computation.18 | loop fusion | flops 2097151 | bytes 1048581 | tf_op jit(solution)/shard_map/reduce_sum | solution.py:35
  58.2 2.1 %fusion.15 = f32[512,512]{1,0:T(8,128)S(1)} fusion(f32[]{:T(128)S(6)} %div.14, f32[256,512]{1,0:T(8,128)S(1)} %broadcast_select_fusion, f32[256,512]{1,0:T(8,128)S(1)} %convert_element_type.20, pred[]{:T(512)S(6)} %eq.24), kind=kOutput, calls=%fused_computation.24 | convolution fusion | flops 1613234176 | bytes 2097157 | tf_op jit(solution)/shard_map/dot_general | solution.py:19
  60.3 1.9 %fusion.7 = f32[512,512]{1,0:T(8,128)S(1)} fusion(f32[]{:T(128)S(6)} %div.14, f32[]{:T(128)S(6)} %sqrt.11, f32[256,512]{1,0:T(8,128)S(1)} %broadcast_select_fusion, f32[256,512]{1,0:T(8,128)S(1)} %convert_element_type.20, pred[]{:T(512)S(6)} %eq.24), kind=kOutput, calls=%fused_computation.16 | convolution fusion | flops 1613758464 | bytes 2097161 | tf_op jit(solution)/shard_map/dot_general | solution.py:19
  62.3 1.8 %fusion.61 = f32[512,512]{1,0:T(8,128)S(1)} fusion(f32[512,512]{1,0:T(8,128)S(1)} %fusion.15), kind=kOutput, calls=%fused_computation.73 | convolution fusion | flops 1610612736 | bytes 2097152 | tf_op jit(solution)/shard_map/dot_general | solution.py:19
  64.1 1.9 %fusion.9 = f32[512,512]{1,0:T(8,128)S(1)} fusion(f32[512,512]{1,0:T(8,128)S(1)} %fusion.61, f32[]{:T(128)S(6)} %div.14, f32[256,512]{1,0:T(8,128)S(1)} %broadcast_select_fusion, f32[256,512]{1,0:T(8,128)S(1)} %convert_element_type.20, pred[]{:T(512)S(6)} %eq.24), kind=kOutput, calls=%fused_computation.20 | convolution fusion | flops 1612447744 | bytes 3145733 | tf_op jit(solution)/shard_map/dot_general | solution.py:19
  66.1 1.9 %fusion.11 = f32[512,512]{1,0:T(8,128)S(1)} fusion(f32[512,512]{1,0:T(8,128)S(1)} %fusion.9), kind=kOutput, calls=%fused_computation.22 | convolution fusion | flops 1611661312 | bytes 2097152 | tf_op jit(solution)/shard_map/dot_general | solution.py:19
  68.0 1.9 %fusion.13 = f32[512,512]{1,0:T(8,128)S(1)} fusion(f32[512,512]{1,0:T(8,128)S(1)} %fusion.7, f32[512,512]{1,0:T(8,128)S(1)} %fusion.9), kind=kOutput, calls=%fused_computation.23 | convolution fusion | flops 1611661312 | bytes 3145728 | tf_op jit(solution)/shard_map/dot_general | solution.py:19
  69.9 2.1 %fusion.62 = f32[512,512]{1,0:T(8,128)S(1)} fusion(f32[512,512]{1,0:T(8,128)S(1)} %fusion.11), kind=kOutput, calls=%fused_computation.74 | convolution fusion | flops 1610612736 | bytes 2097152 | tf_op jit(solution)/shard_map/dot_general | solution.py:19
  72.0 1.9 %fusion = f32[512,512]{1,0:T(8,128)S(1)} fusion(f32[512,512]{1,0:T(8,128)S(1)} %fusion.62, f32[512,512]{1,0:T(8,128)S(1)} %fusion.9), kind=kOutput, calls=%fused_computation.3 | convolution fusion | flops 1611661312 | bytes 3145728 | tf_op jit(solution)/shard_map/dot_general | solution.py:19
  73.9 1.9 %convolution_convert_fusion = bf16[512,512]{1,0:T(8,128)(2,1)S(1)} fusion(f32[512,512]{1,0:T(8,128)S(1)} %fusion.13, f32[512,512]{1,0:T(8,128)S(1)} %fusion), kind=kOutput, calls=%fused_computation.4 | convolution fusion | flops 1610874880 | bytes 2621440 | tf_op jit(solution)/shard_map/dot_general | solution.py:19
  75.7 0.0 copy-start.4
  75.7 0.0 copy-start.6
  75.8 2.4 %collective-permute-start.3 = (bf16[256,512]{1,0:T(8,128)(2,1)S(1)}, bf16[256,512]{1,0:T(8,128)(2,1)S(1)}, u32[]{:S(2)}, u32[]{:S(2)}) collective-permute-start(bf16[256,512]{1,0:T(8,128)(2,1)S(1)} %constant_dynamic-slice_fusion), channel_id=1, source_target_pairs={{0,1},{1,0},{2,3},{3,2},{4,5},{5,4},{6,7},{7,6},{8,9},{9,8},{10,11... | collective-permute-start | bytes 786440 | tf_op jit(solution)/shard_map/ppermute | solution.py:15
  78.2 0.0 copy-start.8
  78.2 0.6 copy-done.8
  78.8 0.6 compare_reduce_fusion
  79.5 0.0 collective-permute-done.3
  79.5 0.0 copy-done.4
  79.5 0.0 copy-done.6
  79.5 1.5 %fusion.42 = (bf16[1,256,512]{2,1,0:T(8,128)(2,1)}, bf16[1,256,512]{2,1,0:T(8,128)(2,1)}) fusion(bf16[1,256,512]{2,1,0:T(8,128)(2,1)S(1)} %copy-done.6, bf16[256,512]{1,0:T(8,128)(2,1)S(1)} %collective-permute-done.3, pred[]{:T(512)S(6)} %eq.24, pred[]{:T(512)} %compare_reduce_fusion, bf16[512,512]{1,0:T(8,128)(2,1)S(1)} %convolution_convert_fusion, ...), kind=kLoop, calls=%fused_computation.53 | loop fusion | flops 524288 | bytes 1572870 | tf_op jit(solution)/shard_map/broadcast_in_dim | solution.py:104
  81.0 0.0 all-to-all-done.1
  81.0 0.7 copy.14
  (2 shorter events, 0.1 us)
Async XLA Ops:
  2.3 16.9 %copy-start.3 = (bf16[1,256,512]{2,1,0:T(8,128)(2,1)S(1)}, bf16[1,256,512]{2,1,0:T(8,128)(2,1)}, u32[]{:S(2)}) copy-start(bf16[1,256,512]{2,1,0:T(8,128)(2,1)} %param.9) | copy-start | bytes 786436
  2.3 42.9 %copy-start.5 = (bf16[1,256,512]{2,1,0:T(8,128)(2,1)S(1)}, bf16[1,256,512]{2,1,0:T(8,128)(2,1)}, u32[]{:S(2)}) copy-start(bf16[1,256,512]{2,1,0:T(8,128)(2,1)} %param.10) | copy-start | bytes 786436
  2.3 38.9 %all-to-all-start = ((bf16[16,32,256]{2,0,1:T(8,128)(2,1)}), bf16[16,32,256]{2,0,1:T(8,128)(2,1)S(1)}, u32[]{:S(2)}, u32[]{:S(2)}) async-start(bf16[16,32,256]{2,0,1:T(8,128)(2,1)} %bitcast.45), calls=%async_computation | async-start | bytes 524288 | tf_op jit(solution)/shard_map/all_to_all | solution.py:56
  19.2 24.9 %collective-permute-start = (bf16[256,512]{1,0:T(8,128)(2,1)S(1)}, bf16[256,512]{1,0:T(8,128)(2,1)S(1)}, u32[]{:S(2)}, u32[]{:S(2)}) collective-permute-start(bf16[256,512]{1,0:T(8,128)(2,1)S(1)} %bitcast.53), channel_id=1, source_target_pairs={{0,1},{1,0},{2,3},{3,2},{4,5},{5,4},{6,7},{7,6},{8,9},{9,8},{10,11... | collective-permute-start | bytes 786440 | tf_op jit(solution)/shard_map/ppermute | solution.py:15
  41.2 4.0 %collective-permute-start.1 = (bf16[512,256]{1,0:T(8,128)(2,1)S(1)}, bf16[512,256]{1,0:T(8,128)(2,1)S(1)}, u32[]{:S(2)}, u32[]{:S(2)}) collective-permute-start(bf16[512,256]{1,0:T(8,128)(2,1)S(1)} %bitcast.49), channel_id=1, source_target_pairs={{0,1},{1,0},{2,3},{3,2},{4,5},{5,4},{6,7},{7,6},{8,9},{9,8},{10,11... | collective-permute-start | bytes 786440 | tf_op jit(solution)/shard_map/ppermute | solution.py:15
  46.7 34.3 %all-to-all-start.1 = ((bf16[32,16,256]{2,1,0:T(8,128)(2,1)}), bf16[32,16,256]{2,1,0:T(8,128)(2,1)S(1)}, u32[]{:S(2)}, u32[]{:S(2)}) async-start(bf16[32,16,256]{2,1,0:T(8,128)(2,1)} %bitcast.5), calls=%async_computation.1 | async-start | bytes 524288 | tf_op jit(solution)/shard_map/all_to_all | solution.py:84
  50.6 1.0 %copy-start.7 = (f32[1,256,512]{2,1,0:T(8,128)S(1)}, f32[1,256,512]{2,1,0:T(8,128)}, u32[]{:S(2)}) copy-start(f32[1,256,512]{2,1,0:T(8,128)} %param.8) | copy-start | bytes 1572868
  51.7 1.0 %copy-start.2 = (f32[1,256,512]{2,1,0:T(8,128)S(1)}, f32[1,256,512]{2,1,0:T(8,128)}, u32[]{:S(2)}) copy-start(f32[1,256,512]{2,1,0:T(8,128)} %param.7) | copy-start | bytes 1572868
  52.7 2.8 %copy-start = (f32[256,512]{1,0:T(8,128)}, f32[256,512]{1,0:T(8,128)S(1)}, u32[]{:S(2)}) copy-start(f32[256,512]{1,0:T(8,128)S(1)} %fusion.2) | copy-start | bytes 1572868
  53.1 2.6 %copy-start.1 = (f32[256,512]{1,0:T(8,128)}, f32[256,512]{1,0:T(8,128)S(1)}, u32[]{:S(2)}) copy-start(f32[256,512]{1,0:T(8,128)S(1)} %get-tuple-element.8) | copy-start | bytes 1572868
  53.1 3.4 %collective-permute-start.2 = (bf16[256,512]{1,0:T(8,128)(2,1)S(1)}, bf16[256,512]{1,0:T(8,128)(2,1)S(1)}, u32[]{:S(2)}, u32[]{:S(2)}) collective-permute-start(bf16[256,512]{1,0:T(8,128)(2,1)S(1)} %get-tuple-element.7), channel_id=1, source_target_pairs={{0,1},{1,0},{2,3},{3,2},{4,5},{5,4},{6,7},{7,6},{8,9},{9,8},{10,11... | collective-permute-start | bytes 786440 | tf_op jit(solution)/shard_map/ppermute | solution.py:15
  75.7 3.8 %copy-start.4 = (bf16[1,256,512]{2,1,0:T(8,128)(2,1)S(1)}, bf16[1,256,512]{2,1,0:T(8,128)(2,1)}, u32[]{:S(2)}) copy-start(bf16[1,256,512]{2,1,0:T(8,128)(2,1)} %param.9) | copy-start | bytes 786436
  75.7 3.8 %copy-start.6 = (bf16[1,256,512]{2,1,0:T(8,128)(2,1)S(1)}, bf16[1,256,512]{2,1,0:T(8,128)(2,1)}, u32[]{:S(2)}) copy-start(bf16[1,256,512]{2,1,0:T(8,128)(2,1)} %param.10) | copy-start | bytes 786436
  75.8 3.7 %collective-permute-start.3 = (bf16[256,512]{1,0:T(8,128)(2,1)S(1)}, bf16[256,512]{1,0:T(8,128)(2,1)S(1)}, u32[]{:S(2)}, u32[]{:S(2)}) collective-permute-start(bf16[256,512]{1,0:T(8,128)(2,1)S(1)} %constant_dynamic-slice_fusion), channel_id=1, source_target_pairs={{0,1},{1,0},{2,3},{3,2},{4,5},{5,4},{6,7},{7,6},{8,9},{9,8},{10,11... | collective-permute-start | bytes 786440 | tf_op jit(solution)/shard_map/ppermute | solution.py:15
  78.2 0.7 copy-start.8
where the time goes:
time: 82.3 us; the launch traced here: 81.7 us
  starting transfers between devices  30.6 us (37%)
  waiting for transfers between devices  21.8 us (26%)
  matrix products  19.6 us (24%)
  local copies, waits for them, and re-layouts  4.69 us (6%)
  other arithmetic  3.3 us (4%)
  between operations  1.7 us (2%)
    all_to_all x1, waiting for transfers between devices, body(): lax.all_to_all(gradient, 'bcol', split_axis=1, concat_axis=0, tiled=True)  19.8 us
    dot_general x9, matrix products, product(): return jnp.dot(left_side, right_side, precision=highest)  17.4 us
    all_to_all x1, starting transfers between devices, body(): lax.all_to_all(gradient, 'bcol', split_axis=1, concat_axis=0, tiled=True)  16.9 us
    ppermute x4, starting transfers between devices, from_partner(): lax.ppermute(shard, axis, [(i, i ^ 1 << stride) for i in range(lax.axis_s...  9.87 us
    all_to_all x1, starting transfers between devices, body(): lax.all_to_all(update_cols, 'bcol', split_axis=0, concat_axis=1, tiled=True)  3.89 us
    unnamed x18, local copies, waits for them, and re-layouts  2.28 us
    ppermute x4, waiting for transfers between devices, from_partner(): lax.ppermute(shard, axis, [(i, i ^ 1 << stride) for i in range(lax.axis_s...  1.98 us
    all_to_all x1, local copies, waits for them, and re-layouts, body(): lax.all_to_all(gradient, 'bcol', split_axis=1, concat_axis=0, tiled=True)  1.67 us
  transfers between devices with their start and end apart: 6, of which 3 were waited for; matrix products, arithmetic and copies ran while one was open for 26% of the time, Pallas kernels for 0%

commit v1 on v0

v1 whole, which is shorter than its diff:
```python
import functools

import jax
import jax.numpy as jnp
from jax import lax
from jax.experimental import pallas as pl
from jax.experimental.pallas import tpu as pltpu
from jax.sharding import PartitionSpec as P

MESH = pl.DeviceIdType.MESH
bf16 = jnp.bfloat16
f32 = jnp.float32

decay = 0.9
epsilon = 1e-06
LEAD = 1.25

ROWS_BY_ROWS = (((1,), (1,)), ((), ()))
COLS_BY_COLS = (((0,), (0,)), ((), ()))


def product(left_side, right_side):
    return jnp.dot(left_side, right_side, preferred_element_type=f32)


def root_into(root_ref, stat_ref, held):
    moment, lead, tail, m16, n16, h16, p16, v16, q16 = held
    size = stat_ref.shape[0]
    a = LEAD
    diagonal = lax.broadcasted_iota(jnp.int32, (size, size), 0) == lax.broadcasted_iota(
        jnp.int32, (size, size), 1
    )
    shifted = stat_ref[...] + jnp.where(diagonal, epsilon, 0.0)
    total = jnp.sum(jnp.sum(shifted * shifted, axis=0, keepdims=True), axis=1, keepdims=True)
    scaling = 2.5 / jnp.sqrt(total)
    scale = jnp.sqrt(jnp.sqrt(scaling))
    moment[...] = shifted * scaling
    m16[...] = moment[...].astype(bf16)
    tail[...] = product(m16[...], m16[...])
    lead[...] = a * moment[...] - 0.25 * tail[...]
    h16[...] = lead[...].astype(bf16)
    tail[...] = 0.0625 * tail[...] - (0.5 * a) * moment[...]
    n16[...] = tail[...].astype(bf16)
    p16[...] = (2.0 * a * a * tail[...] + product(n16[...], n16[...])).astype(bf16)
    tail[...] = -0.25 * (a * moment[...] + a**4 * lead[...] + product(p16[...], h16[...]))
    v16[...] = tail[...].astype(bf16)
    q16[...] = (2.0 * a * a * tail[...] + product(v16[...], v16[...])).astype(bf16)
    lead[...] = a * a * moment[...] + product(v16[...], m16[...])
    h16[...] = lead[...].astype(bf16)
    lead[...] = a**4 * lead[...] + product(q16[...], h16[...])
    h16[...] = lead[...].astype(bf16)
    lead[...] = a**4 * lead[...] + product(q16[...], h16[...])
    root = jnp.where(diagonal, a**3, 0.0) + a * tail[...] - 0.25 * lead[...]
    root_ref[...] = (scale * root).astype(bf16)


def step_kernel(
    grad, left_stats, right_stats, left_roots, right_roots,
    update, new_left, new_right, fresh_left, fresh_right,
    block, left_some, right_whole, stat, other, mixed, cols, root, taken,
    moment, lead, tail, m16, n16, h16, p16, v16, q16,
    in_send, in_recv, pass_send, pass_recv, out_send, out_recv,
    pair_send, pair_recv, local_sem,
):
    slabs, slab_rows, size = block.shape
    chips, half_rows = slabs // 2, size // 2
    per_half = chips // 2
    me = lax.axis_index("bcol")
    chip, half = lax.div(me, 2), lax.rem(me, 2)
    partner = 2 * chip + (1 - half)
    near = [d * s for d in range(1, chips // 2) for s in (1, -1)] + [chips // 2]

    def peer(offset):
        return lax.rem(chip + (offset + chips), chips)

    def remote(src, dst, send, recv, target):
        return pltpu.make_async_remote_copy(
            src_ref=src, dst_ref=dst, send_sem=send, recv_sem=recv,
            device_id={"bcol": target}, device_id_type=MESH,
        )

    def columns(index):
        return pl.ds(pl.multiple_of(index * size, size), size)

    def rows_of(index):
        return pl.ds(pl.multiple_of(index * half_rows, half_rows), half_rows)

    barrier = pltpu.get_barrier_semaphore()
    for offset in near:
        pl.semaphore_signal(
            barrier, inc=1, device_id={"bcol": 2 * peer(offset) + half}, device_id_type=MESH
        )
    pl.semaphore_signal(barrier, inc=1, device_id={"bcol": partner}, device_id_type=MESH)

    own_block = pltpu.make_async_copy(grad.at[:, columns(chip)], block.at[me], local_sem.at[0])
    own_left = pltpu.make_async_copy(
        left_roots.at[:, half], left_some.at[pl.ds(half * per_half, per_half)], local_sem.at[1]
    )
    own_right = pltpu.make_async_copy(right_roots, right_whole.at[rows_of(half)], local_sem.at[2])
    own_block.start()
    own_left.start()
    own_right.start()

    @pl.when(half == 0)
    def _():
        pltpu.make_async_copy(left_stats, stat.at[rows_of(half)], local_sem.at[3]).start()
        pltpu.make_async_copy(right_stats, other, local_sem.at[4]).start()

    @pl.when(half == 1)
    def _():
        pltpu.make_async_copy(right_stats, stat.at[rows_of(half)], local_sem.at[3]).start()
        pltpu.make_async_copy(left_stats, other, local_sem.at[4]).start()

    pl.semaphore_wait(barrier, chips)

    def in_copy(to, sender):
        return remote(
            grad.at[:, columns(to)], block.at[2 * sender + half],
            in_send.at[to], in_recv.at[sender], 2 * to + half,
        )

    for offset in near[::-1]:
        in_copy(peer(offset), chip).start()

    pair_own = remote(
        grad.at[:, columns(chip)], block.at[me], pass_send.at[chip], pass_recv.at[chip], partner
    )
    pair_right = remote(
        right_roots, right_whole.at[rows_of(half)], pair_send.at[0], pair_recv.at[0], partner
    )
    pair_left = remote(
        left_roots.at[:, 1 - half], left_some.at[pl.ds(half * per_half, per_half)],
        pair_send.at[1], pair_recv.at[1], partner,
    )

    def pair_stat(source):
        return remote(source, stat.at[rows_of(half)], pair_send.at[2], pair_recv.at[2], partner)

    pair_own.start()
    pair_right.start()
    pair_left.start()

    @pl.when(half == 0)
    def _():
        pair_stat(right_stats).start()

    @pl.when(half == 1)
    def _():
        pair_stat(left_stats).start()

    def pass_on(sender):
        slot = block.at[2 * sender + half]
        return remote(slot, slot, pass_send.at[sender], pass_recv.at[sender], partner)

    def passed(sender):
        slot = block.at[2 * sender + (1 - half)]
        return remote(slot, slot, pass_send.at[sender], pass_recv.at[sender], partner)

    for offset in near:
        sender = peer(offset)
        in_copy(sender, sender).wait_recv()
        pass_on(sender).start()

    own_right.wait()
    own_left.wait()
    own_block.wait()
    remote(
        right_roots, right_whole.at[rows_of(1 - half)], pair_send.at[0], pair_recv.at[0], partner
    ).wait_recv()
    remote(
        left_roots.at[:, 1 - half], left_some.at[pl.ds((1 - half) * per_half, per_half)],
        pair_send.at[1], pair_recv.at[1], partner,
    ).wait_recv()
    passed(chip).wait_recv()
    for offset in near:
        passed(peer(offset)).wait_recv()

    whole = block[...].reshape(size, size)
    mixed[...] = product(whole, right_whole[...]).astype(bf16)
    cols[...] = (
        product(left_some[...].reshape(half_rows, size), mixed[...])
        .astype(bf16)
        .reshape(cols.shape)
    )

    def out_copy(to, sender):
        return remote(
            cols.at[to], update.at[:, columns(sender)], out_send.at[to], out_recv.at[sender],
            2 * to + half,
        )

    for offset in near[::-1]:
        out_copy(peer(offset), chip).start()
    keep = pltpu.make_async_copy(cols.at[chip], update.at[:, columns(chip)], local_sem.at[5])
    keep.start()

    remote(
        left_stats, stat.at[rows_of(1 - half)], pair_send.at[2], pair_recv.at[2], partner
    ).wait_recv()
    pltpu.make_async_copy(left_stats, stat.at[rows_of(half)], local_sem.at[3]).wait()
    pltpu.make_async_copy(right_stats, other, local_sem.at[4]).wait()

    def blend(old, gram):
        return decay * old + (1.0 - decay) * gram

    @pl.when(half == 0)
    def _():
        g = block[...].reshape(size, size)
        stat[...] = blend(
            stat[...], lax.dot_general(g, g, ROWS_BY_ROWS, preferred_element_type=f32)
        )
        new_left[...] = stat[:half_rows]
        new_right[...] = blend(
            other[...],
            lax.dot_general(g[:, :half_rows], g, COLS_BY_COLS, preferred_element_type=f32),
        )

    @pl.when(half == 1)
    def _():
        g = block[...].reshape(size, size)
        stat[...] = blend(
            stat[...], lax.dot_general(g, g, COLS_BY_COLS, preferred_element_type=f32)
        )
        new_right[...] = stat[half_rows:]
        new_left[...] = blend(
            other[...],
            lax.dot_general(g[half_rows:], g, ROWS_BY_ROWS, preferred_element_type=f32),
        )

    root_into(root, stat, (moment, lead, tail, m16, n16, h16, p16, v16, q16))
    give = remote(root.at[rows_of(1 - half)], taken, pair_send.at[3], pair_recv.at[3], partner)
    give.start()

    @pl.when(half == 0)
    def _():
        fresh_left[...] = root[:half_rows]

    @pl.when(half == 1)
    def _():
        fresh_right[...] = root[half_rows:]

    give.wait_recv()

    @pl.when(half == 0)
    def _():
        fresh_right[...] = taken[...]

    @pl.when(half == 1)
    def _():
        fresh_left[...] = taken[...]

    keep.wait()
    for offset in near:
        out_copy(peer(offset), peer(offset)).wait_recv()
    for offset in near:
        in_copy(peer(offset), chip).wait_send()
        pass_on(peer(offset)).wait_send()
        out_copy(peer(offset), chip).wait_send()
    pair_own.wait_send()
    pair_right.wait_send()
    pair_left.wait_send()
    pair_stat(left_stats).wait_send()
    give.wait_send()


def final_kernel(
    refresh, update, new_left, new_right, fresh_left, fresh_right, old_left, old_right,
    update_out, left_out, right_out, left_root, right_root, chosen, sems,
):
    block_col = lax.div(lax.axis_index("bcol"), 2)
    fetched = pltpu.make_async_copy(refresh, chosen, sems.at[5])
    fetched.start()
    sure = [
        pltpu.make_async_copy(update, update_out, sems.at[0]),
        pltpu.make_async_copy(new_left, left_out, sems.at[1]),
        pltpu.make_async_copy(new_right, right_out, sems.at[2]),
    ]
    for copy in sure:
        copy.start()
    fetched.wait()
    listed = chosen[0, 0] == block_col
    for place in range(1, chosen.shape[1]):
        listed = jnp.logical_or(listed, chosen[0, place] == block_col)

    @pl.when(listed)
    def _():
        pltpu.make_async_copy(fresh_left, left_root, sems.at[3]).start()
        pltpu.make_async_copy(fresh_right, right_root, sems.at[4]).start()

    @pl.when(jnp.logical_not(listed))
    def _():
        pltpu.make_async_copy(old_left, left_root, sems.at[3]).start()
        pltpu.make_async_copy(old_right, right_root, sems.at[4]).start()

    for copy in sure:
        copy.wait()
    pltpu.make_async_copy(fresh_left, left_root, sems.at[3]).wait()
    pltpu.make_async_copy(fresh_right, right_root, sems.at[4]).wait()


def body(chips, gradient, left_stats, right_stats, left_roots, right_roots, refresh):
    slab_rows, half_rows, size = gradient.shape[0], left_stats.shape[1], left_stats.shape[2]
    width = gradient.shape[1]
    per_half = chips // 2
    place = functools.partial(pltpu.with_memory_space_constraint, memory_space=pltpu.HBM)
    in_hbm = pl.BlockSpec(memory_space=pltpu.HBM)
    in_vmem = pl.BlockSpec(memory_space=pltpu.VMEM)
    shaped = jax.ShapeDtypeStruct
    dma = pltpu.SemaphoreType.DMA
    square32, square16 = pltpu.VMEM((size, size), f32), pltpu.VMEM((size, size), bf16)
    stat_half = shaped((half_rows, size), f32)
    root_half = shaped((half_rows, size), bf16)
    results = pl.pallas_call(
        step_kernel,
        out_shape=(shaped((slab_rows, width), bf16), stat_half, stat_half, root_half, root_half),
        in_specs=[in_hbm] * 5,
        out_specs=[in_vmem] * 5,
        scratch_shapes=[
            pltpu.VMEM((2 * chips, slab_rows, size), bf16),
            pltpu.VMEM((chips, slab_rows, size), bf16),
            square16,
            square32,
            pltpu.VMEM((half_rows, size), f32),
            square16,
            pltpu.VMEM((chips, slab_rows, size), bf16),
            square16,
            pltpu.VMEM((half_rows, size), bf16),
            square32, square32, square32,
            square16, square16, square16, square16, square16, square16,
            dma((chips,)), dma((chips,)), dma((chips,)), dma((chips,)),
            dma((chips,)), dma((chips,)), dma((4,)), dma((4,)), dma((6,)),
        ],
        compiler_params=pltpu.CompilerParams(
            collective_id=0, has_side_effects=True, vmem_limit_bytes=40 * 2**20
        ),
        name="exchange",
    )(
        place(gradient),
        place(left_stats[0]),
        place(right_stats[0]),
        place(left_roots.reshape(per_half, 2, slab_rows, size)),
        place(right_roots[0]),
    )
    outputs = pl.pallas_call(
        final_kernel,
        out_shape=(shaped((slab_rows, width), bf16), stat_half, stat_half, root_half, root_half),
        in_specs=[in_hbm] + [pl.BlockSpec(memory_space=pl.ANY)] * 5 + [in_hbm] * 2,
        out_specs=[in_hbm] * 5,
        scratch_shapes=[pltpu.SMEM(refresh.shape, jnp.int32), dma((6,))],
        compiler_params=pltpu.CompilerParams(vmem_limit_bytes=2**20),
        name="place",
    )(place(refresh), *results, place(left_roots[0]), place(right_roots[0]))
    return (outputs[0],) + tuple(out[None] for out in outputs[1:])


def solution(mesh):
    rows, blocks = P(("brow", "bcol"), None), P("brow", "bcol", None)
    return jax.shard_map(
        functools.partial(body, mesh.shape["bcol"] // 2),
        mesh=mesh,
        in_specs=(rows, blocks, blocks, blocks, blocks, P("brow", None)),
        out_specs=(rows, blocks, blocks, blocks, blocks),
        check_vma=False,
    )
```

time: 82.3 us -> 64.1 us (0.78)
  Pallas kernels: 0 us -> 63.4 us
  starting transfers between devices: 30.6 us -> 0 us
  waiting for transfers between devices: 21.8 us -> 0 us
  matrix products: 19.6 us -> 0 us
  local copies, waits for them, and re-layouts: 4.69 us -> 0 us
  other arithmetic: 3.3 us -> 0 us
  between operations: 1.7 us -> 0.64 us
    pallas_call x0 -> x2, Pallas kernels: none -> 63.4 us  [the longest x1 45.7 us: body(): pl.pallas_call(step_kernel, out_shape=(shaped((slab_rows, width), bf16),...]
    all_to_all x2 -> x0, starting transfers between devices: 20.8 us -> none  [the longest x1 16.9 us: body(): lax.all_to_all(gradient, 'bcol', split_axis=1, concat_axis=0, tiled=True)]
    all_to_all x2 -> x0, waiting for transfers between devices: 19.8 us -> none  [the longest x1 19.8 us: body(): lax.all_to_all(gradient, 'bcol', split_axis=1, concat_axis=0, tiled=True)]
    dot_general x12 -> x0, matrix products: 19.6 us -> none  [the longest x9 17.4 us: product(): return jnp.dot(left_side, right_side, precision=highest)]
    ppermute x4 -> x0, starting transfers between devices: 9.87 us -> none  [from_partner(): lax.ppermute(shard, axis, [(i, i ^ 1 << stride) for i in range(lax.axis_s...]
    all_to_all x2 -> x0, local copies, waits for them, and re-layouts: 2.39 us -> none  [the longest x1 1.67 us: body(): lax.all_to_all(gradient, 'bcol', split_axis=1, concat_axis=0, tiled=True)]
    unnamed x18 -> x0, local copies, waits for them, and re-layouts: 2.28 us -> none
    ppermute x4 -> x0, waiting for transfers between devices: 1.98 us -> none  [from_partner(): lax.ppermute(shard, axis, [(i, i ^ 1 << stride) for i in range(lax.axis_s...]
  transfers between devices with their start and end apart: 6 -> 0, of which waited for: 3 -> 0; matrix products, arithmetic and copies ran while one was open for 26% -> 0% of each run, Pallas kernels for 0% -> 0%
where the time goes in v1:
time: 64.1 us; the launch traced here: 64 us
  Pallas kernels  63.4 us (99%)
    pallas_call x1, Pallas kernels, body(): pl.pallas_call(step_kernel, out_shape=(shaped((slab_rows, width), bf16),...  45.7 us
    pallas_call x1, Pallas kernels, body(): pl.pallas_call(final_kernel, out_shape=(shaped((slab_rows, width), bf16),...  17.7 us

profile of v1, /device:TPU:1, one launch (start us, length us, event | category | flops | bytes accessed | tf_op | source)
XLA Modules:
  0.0 64.0 jit_solution(3833303500237431384)
XLA Ops:
  0.6 45.7 %exchange.1 = (bf16[16,8192]{1,0:T(8,128)(2,1)S(1)}, f32[256,512]{1,0:T(8,128)S(1)}, f32[256,512]{1,0:T(8,128)S(1)}, bf16[256,512]{1,0:T(8,128)(2,1)S(1)}, bf16[256,512]{1,0:T(8,128)(2,1)S(1)}) custom-call(bf16[16,8192]{1,0:T(8,128)(2,1)} %grad.1, f32[256,512]{1,0:T(8,128)} %bitcast.13, f32[256,512]{1,0:T(8,128)} %bitcast.14, ...), custom_call_target="tpu_custom_call" | custom-call | tf_op jit(solution)/shard_map/exchange/pallas_call | solution.py:313
  46.3 17.7 %place.1 = (bf16[16,8192]{1,0:T(8,128)(2,1)}, f32[256,512]{1,0:T(8,128)}, f32[256,512]{1,0:T(8,128)}, bf16[256,512]{1,0:T(8,128)(2,1)}, bf16[256,512]{1,0:T(8,128)(2,1)}) custom-call(s32[1,4]{1,0:T(1,128)} %refresh.1, bf16[16,8192]{1,0:T(8,128)(2,1)S(1)} %get-tuple-element.15.update, f32[256,512]{1,0:T(8,128)S(1)} %get-tuple-element.16.new_left, ...), custom_call_target="tpu_custom_call" | custom-call | tf_op jit(solution)/shard_map/place/pallas_call | solution.py:344

commit v2 on v1

--- a/solution.py
+++ b/solution.py
@@ -79,6 +79,16 @@
             device_id={"bcol": target}, device_id_type=MESH,
         )
 
+    def in_turn(send, first):
+        for parity in (0, 1):
+
+            @pl.when(lax.rem(chip, 2) == parity)
+            def _():
+                for turn in (first, 1 - first):
+                    for offset in near[::-1]:
+                        if (parity + offset) % 2 == turn:
+                            send(peer(offset))
+
     def columns(index):
         return pl.ds(pl.multiple_of(index * size, size), size)
 
@@ -119,8 +129,7 @@
             in_send.at[to], in_recv.at[sender], 2 * to + half,
         )
 
-    for offset in near[::-1]:
-        in_copy(peer(offset), chip).start()
+    in_turn(lambda to: in_copy(to, chip).start(), 0)
 
     pair_own = remote(
         grad.at[:, columns(chip)], block.at[me], pass_send.at[chip], pass_recv.at[chip], partner
@@ -156,7 +165,7 @@
         slot = block.at[2 * sender + (1 - half)]
         return remote(slot, slot, pass_send.at[sender], pass_recv.at[sender], partner)
 
-    for offset in near:
+    for offset in near[::-1]:
         sender = peer(offset)
         in_copy(sender, sender).wait_recv()
         pass_on(sender).start()
@@ -189,8 +198,7 @@
             2 * to + half,
         )
 
-    for offset in near[::-1]:
-        out_copy(peer(offset), chip).start()
+    in_turn(lambda to: out_copy(to, chip).start(), 0)
     keep = pltpu.make_async_copy(cols.at[chip], update.at[:, columns(chip)], local_sem.at[5])
     keep.start()
 
@@ -344,12 +352,12 @@
     outputs = pl.pallas_call(
         final_kernel,
         out_shape=(shaped((slab_rows, width), bf16), stat_half, stat_half, root_half, root_half),
-        in_specs=[in_hbm] + [pl.BlockSpec(memory_space=pl.ANY)] * 5 + [in_hbm] * 2,
+        in_specs=[in_hbm] + [pl.BlockSpec(memory_space=pl.ANY)] * 7,
         out_specs=[in_hbm] * 5,
         scratch_shapes=[pltpu.SMEM(refresh.shape, jnp.int32), dma((6,))],
         compiler_params=pltpu.CompilerParams(vmem_limit_bytes=2**20),
         name="place",
-    )(place(refresh), *results, place(left_roots[0]), place(right_roots[0]))
+    )(place(refresh), *results, left_roots[0], right_roots[0])
     return (outputs[0],) + tuple(out[None] for out in outputs[1:])
 
 

time: 64.1 us -> 47.4 us (0.74)
  the two profiles are of different devices: /device:TPU:1 before, /device:TPU:59 now
where the time goes in v2:
time: 47.4 us; the launch traced here: 47.3 us
  Pallas kernels  46.6 us (98%)
  between operations  0.67 us (1%)
    pallas_call x1, Pallas kernels, body(): pl.pallas_call(step_kernel, out_shape=(shaped((slab_rows, width), bf16),...  45.1 us
    pallas_call x1, Pallas kernels, body(): pl.pallas_call(final_kernel, out_shape=(shaped((slab_rows, width), bf16),...  1.51 us

profile of v2, /device:TPU:59, one launch (start us, length us, event | category | flops | bytes accessed | tf_op | source)
XLA Modules:
  0.0 47.3 jit_solution(17428683122554880848)
XLA Ops:
  0.6 0.0 copy-start
  0.6 0.0 copy-start.1
  0.7 45.1 %exchange.1 = (bf16[16,8192]{1,0:T(8,128)(2,1)S(1)}, f32[256,512]{1,0:T(8,128)S(1)}, f32[256,512]{1,0:T(8,128)S(1)}, bf16[256,512]{1,0:T(8,128)(2,1)S(1)}, bf16[256,512]{1,0:T(8,128)(2,1)S(1)}) custom-call(bf16[16,8192]{1,0:T(8,128)(2,1)} %grad.1, f32[256,512]{1,0:T(8,128)} %bitcast.13, f32[256,512]{1,0:T(8,128)} %bitcast.14, ...), custom_call_target="tpu_custom_call" | custom-call | tf_op jit(solution)/shard_map/exchange/pallas_call | solution.py:321
  45.8 0.0 copy-done
  45.8 0.0 copy-done.1
  45.8 1.5 %place.1 = (bf16[16,8192]{1,0:T(8,128)(2,1)}, f32[256,512]{1,0:T(8,128)}, f32[256,512]{1,0:T(8,128)}, bf16[256,512]{1,0:T(8,128)(2,1)}, bf16[256,512]{1,0:T(8,128)(2,1)}) custom-call(s32[1,4]{1,0:T(1,128)} %refresh.1, bf16[16,8192]{1,0:T(8,128)(2,1)S(1)} %get-tuple-element.15.update, f32[256,512]{1,0:T(8,128)S(1)} %get-tuple-element.16.new_left, ...), custom_call_target="tpu_custom_call" | custom-call | tf_op jit(solution)/shard_map/place/pallas_call | solution.py:352
Async XLA Ops:
  0.6 45.1 %copy-start = (bf16[1,256,512]{2,1,0:T(8,128)(2,1)S(1)}, bf16[1,256,512]{2,1,0:T(8,128)(2,1)}, u32[]{:S(2)}) copy-start(bf16[1,256,512]{2,1,0:T(8,128)(2,1)} %param.9) | copy-start | bytes 786436
  0.6 45.1 %copy-start.1 = (bf16[1,256,512]{2,1,0:T(8,128)(2,1)S(1)}, bf16[1,256,512]{2,1,0:T(8,128)(2,1)}, u32[]{:S(2)}) copy-start(bf16[1,256,512]{2,1,0:T(8,128)(2,1)} %param.10) | copy-start | bytes 786436

commit v3 on v2

--- a/solution.py
+++ b/solution.py
@@ -13,6 +13,8 @@
 
 decay = 0.9
 epsilon = 1e-06
+IN_FLIGHT = 4
+OUT_FLIGHT = 8
 LEAD = 1.25
 
 ROWS_BY_ROWS = (((1,), (1,)), ((), ()))
@@ -23,7 +25,15 @@
     return jnp.dot(left_side, right_side, preferred_element_type=f32)
 
 
-def root_into(root_ref, stat_ref, held):
+def begins(chips, chip):
+    if 2 * chip < chips:
+        return chip
+    if 4 * chip >= 3 * chips:
+        return 2 * chips - 1 - chip
+    return chips / 2 + chip + 2.4
+
+
+def root_into(root_ref, stat_ref, held, step):
     moment, lead, tail, m16, n16, h16, p16, v16, q16 = held
     size = stat_ref.shape[0]
     a = LEAD
@@ -37,16 +47,21 @@
     moment[...] = shifted * scaling
     m16[...] = moment[...].astype(bf16)
     tail[...] = product(m16[...], m16[...])
+    step()
     lead[...] = a * moment[...] - 0.25 * tail[...]
     h16[...] = lead[...].astype(bf16)
     tail[...] = 0.0625 * tail[...] - (0.5 * a) * moment[...]
     n16[...] = tail[...].astype(bf16)
     p16[...] = (2.0 * a * a * tail[...] + product(n16[...], n16[...])).astype(bf16)
+    step()
     tail[...] = -0.25 * (a * moment[...] + a**4 * lead[...] + product(p16[...], h16[...]))
     v16[...] = tail[...].astype(bf16)
+    step()
     q16[...] = (2.0 * a * a * tail[...] + product(v16[...], v16[...])).astype(bf16)
+    step()
     lead[...] = a * a * moment[...] + product(v16[...], m16[...])
     h16[...] = lead[...].astype(bf16)
+    step()
     lead[...] = a**4 * lead[...] + product(q16[...], h16[...])
     h16[...] = lead[...].astype(bf16)
     lead[...] = a**4 * lead[...] + product(q16[...], h16[...])
@@ -79,15 +94,27 @@
             device_id={"bcol": target}, device_id_type=MESH,
         )
 
-    def in_turn(send, first):
+    def even_first(parity):
+        return [o for turn in (0, 1) for o in near[::-1] if (parity + o) % 2 == turn]
+
+    def gather_rows(copy):
         for parity in (0, 1):
 
             @pl.when(lax.rem(chip, 2) == parity)
             def _():
-                for turn in (first, 1 - first):
-                    for offset in near[::-1]:
-                        if (parity + offset) % 2 == turn:
-                            send(peer(offset))
+                order = even_first(parity)
+                for place, offset in enumerate(order):
+                    if place >= IN_FLIGHT:
+                        copy(peer(order[place - IN_FLIGHT])).wait_send()
+                    copy(peer(offset)).start()
+
+    def gather_rest(copy):
+        for parity in (0, 1):
+
+            @pl.when(lax.rem(chip, 2) == parity)
+            def _():
+                for offset in even_first(parity)[-IN_FLIGHT:]:
+                    copy(peer(offset)).wait_send()
 
     def columns(index):
         return pl.ds(pl.multiple_of(index * size, size), size)
@@ -123,31 +150,31 @@
 
     pl.semaphore_wait(barrier, chips)
 
+    pair_own = remote(
+        grad.at[:, columns(chip)], block.at[me], pass_send.at[chip], pass_recv.at[chip], partner
+    )
+    pair_right = remote(
+        right_roots, right_whole.at[rows_of(half)], pair_send.at[0], pair_recv.at[0], partner
+    )
+    pair_left = remote(
+        left_roots.at[:, 1 - half], left_some.at[pl.ds(half * per_half, per_half)],
+        pair_send.at[1], pair_recv.at[1], partner,
+    )
+
+    def pair_stat(source):
+        return remote(source, stat.at[rows_of(half)], pair_send.at[2], pair_recv.at[2], partner)
+
+    pair_own.start()
+    pair_right.start()
+    pair_left.start()
+
     def in_copy(to, sender):
         return remote(
             grad.at[:, columns(to)], block.at[2 * sender + half],
             in_send.at[to], in_recv.at[sender], 2 * to + half,
         )
 
-    in_turn(lambda to: in_copy(to, chip).start(), 0)
-
-    pair_own = remote(
-        grad.at[:, columns(chip)], block.at[me], pass_send.at[chip], pass_recv.at[chip], partner
-    )
-    pair_right = remote(
-        right_roots, right_whole.at[rows_of(half)], pair_send.at[0], pair_recv.at[0], partner
-    )
-    pair_left = remote(
-        left_roots.at[:, 1 - half], left_some.at[pl.ds(half * per_half, per_half)],
-        pair_send.at[1], pair_recv.at[1], partner,
-    )
-
-    def pair_stat(source):
-        return remote(source, stat.at[rows_of(half)], pair_send.at[2], pair_recv.at[2], partner)
-
-    pair_own.start()
-    pair_right.start()
-    pair_left.start()
+    gather_rows(lambda to: in_copy(to, chip))
 
     @pl.when(half == 0)
     def _():
@@ -198,7 +225,30 @@
             2 * to + half,
         )
 
-    in_turn(lambda to: out_copy(to, chip).start(), 0)
+    def out_step(place):
+        if place >= OUT_FLIGHT:
+            out_left(place - OUT_FLIGHT)
+        if place < chips:
+
+            @pl.when(chip != turns[place])
+            def _():
+                out_copy(turns[place], chip).start()
+
+    def out_left(place):
+        @pl.when(chip != turns[place])
+        def _():
+            out_copy(turns[place], chip).wait_send()
+
+    turns = sorted(range(chips), key=functools.partial(begins, chips))
+    for place in range(OUT_FLIGHT):
+        out_step(place)
+    places = iter(range(OUT_FLIGHT, chips + OUT_FLIGHT))
+
+    def step():
+        place = next(places, None)
+        if place is not None:
+            out_step(place)
+
     keep = pltpu.make_async_copy(cols.at[chip], update.at[:, columns(chip)], local_sem.at[5])
     keep.start()
 
@@ -235,9 +285,12 @@
             lax.dot_general(g[half_rows:], g, ROWS_BY_ROWS, preferred_element_type=f32),
         )
 
-    root_into(root, stat, (moment, lead, tail, m16, n16, h16, p16, v16, q16))
+    step()
+    root_into(root, stat, (moment, lead, tail, m16, n16, h16, p16, v16, q16), step)
     give = remote(root.at[rows_of(1 - half)], taken, pair_send.at[3], pair_recv.at[3], partner)
     give.start()
+    step()
+    step()
 
     @pl.when(half == 0)
     def _():
@@ -247,6 +300,8 @@
     def _():
         fresh_right[...] = root[half_rows:]
 
+    for place in places:
+        out_step(place)
     give.wait_recv()
 
     @pl.when(half == 0)
@@ -261,9 +316,8 @@
     for offset in near:
         out_copy(peer(offset), peer(offset)).wait_recv()
     for offset in near:
-        in_copy(peer(offset), chip).wait_send()
         pass_on(peer(offset)).wait_send()
-        out_copy(peer(offset), chip).wait_send()
+    gather_rest(lambda to: in_copy(to, chip))
     pair_own.wait_send()
     pair_right.wait_send()
     pair_left.wait_send()

time: 47.4 us -> 44.3 us (0.935)
  the two profiles are of different devices: /device:TPU:59 before, /device:TPU:93 now
where the time goes in v3:
time: 44.3 us; the launch traced here: 44.1 us
  Pallas kernels  43.5 us (98%)
  between operations  0.67 us (2%)
    pallas_call x1, Pallas kernels, body(): pl.pallas_call(step_kernel, out_shape=(shaped((slab_rows, width), bf16),...  41.9 us
    pallas_call x1, Pallas kernels, body(): pl.pallas_call(final_kernel, out_shape=(shaped((slab_rows, width), bf16),...  1.51 us

profile of v3, /device:TPU:93, one launch (start us, length us, event | category | flops | bytes accessed | tf_op | source)
XLA Modules:
  0.0 44.1 jit_solution(9132731318395994609)
XLA Ops:
  0.6 0.0 copy-start
  0.6 0.0 copy-start.1
  0.7 41.9 %exchange.1 = (bf16[16,8192]{1,0:T(8,128)(2,1)S(1)}, f32[256,512]{1,0:T(8,128)S(1)}, f32[256,512]{1,0:T(8,128)S(1)}, bf16[256,512]{1,0:T(8,128)(2,1)S(1)}, bf16[256,512]{1,0:T(8,128)(2,1)S(1)}) custom-call(bf16[16,8192]{1,0:T(8,128)(2,1)} %grad.1, f32[256,512]{1,0:T(8,128)} %bitcast.13, f32[256,512]{1,0:T(8,128)} %bitcast.14, ...), custom_call_target="tpu_custom_call" | custom-call | tf_op jit(solution)/shard_map/exchange/pallas_call | solution.py:375
  42.6 0.0 copy-done
  42.6 0.0 copy-done.1
  42.6 1.5 %place.1 = (bf16[16,8192]{1,0:T(8,128)(2,1)}, f32[256,512]{1,0:T(8,128)}, f32[256,512]{1,0:T(8,128)}, bf16[256,512]{1,0:T(8,128)(2,1)}, bf16[256,512]{1,0:T(8,128)(2,1)}) custom-call(s32[1,4]{1,0:T(1,128)} %refresh.1, bf16[16,8192]{1,0:T(8,128)(2,1)S(1)} %get-tuple-element.15.update, f32[256,512]{1,0:T(8,128)S(1)} %get-tuple-element.16.new_left, ...), custom_call_target="tpu_custom_call" | custom-call | tf_op jit(solution)/shard_map/place/pallas_call | solution.py:406
Async XLA Ops:
  0.6 42.0 %copy-start = (bf16[1,256,512]{2,1,0:T(8,128)(2,1)S(1)}, bf16[1,256,512]{2,1,0:T(8,128)(2,1)}, u32[]{:S(2)}) copy-start(bf16[1,256,512]{2,1,0:T(8,128)(2,1)} %param.9) | copy-start | bytes 786436
  0.6 42.0 %copy-start.1 = (bf16[1,256,512]{2,1,0:T(8,128)(2,1)S(1)}, bf16[1,256,512]{2,1,0:T(8,128)(2,1)}, u32[]{:S(2)}) copy-start(bf16[1,256,512]{2,1,0:T(8,128)(2,1)} %param.10) | copy-start | bytes 786436

commit v4 on v3

--- a/solution.py
+++ b/solution.py
@@ -29,8 +29,8 @@
     if 2 * chip < chips:
         return chip
     if 4 * chip >= 3 * chips:
-        return 2 * chips - 1 - chip
-    return chips / 2 + chip + 2.4
+        return 2 * chips - chip - 0.5
+    return chips / 2 + chip
 
 
 def root_into(root_ref, stat_ref, held, step):
@@ -107,6 +107,8 @@
                     if place >= IN_FLIGHT:
                         copy(peer(order[place - IN_FLIGHT])).wait_send()
                     copy(peer(offset)).start()
+                    if place == min(IN_FLIGHT, len(order)) - 1:
+                        share()
 
     def gather_rest(copy):
         for parity in (0, 1):
@@ -134,19 +136,6 @@
         left_roots.at[:, half], left_some.at[pl.ds(half * per_half, per_half)], local_sem.at[1]
     )
     own_right = pltpu.make_async_copy(right_roots, right_whole.at[rows_of(half)], local_sem.at[2])
-    own_block.start()
-    own_left.start()
-    own_right.start()
-
-    @pl.when(half == 0)
-    def _():
-        pltpu.make_async_copy(left_stats, stat.at[rows_of(half)], local_sem.at[3]).start()
-        pltpu.make_async_copy(right_stats, other, local_sem.at[4]).start()
-
-    @pl.when(half == 1)
-    def _():
-        pltpu.make_async_copy(right_stats, stat.at[rows_of(half)], local_sem.at[3]).start()
-        pltpu.make_async_copy(left_stats, other, local_sem.at[4]).start()
 
     pl.semaphore_wait(barrier, chips)
 
@@ -164,9 +153,31 @@
     def pair_stat(source):
         return remote(source, stat.at[rows_of(half)], pair_send.at[2], pair_recv.at[2], partner)
 
-    pair_own.start()
-    pair_right.start()
-    pair_left.start()
+    def share():
+        own_block.start()
+        own_left.start()
+        own_right.start()
+
+        @pl.when(half == 0)
+        def _():
+            pltpu.make_async_copy(left_stats, stat.at[rows_of(half)], local_sem.at[3]).start()
+            pltpu.make_async_copy(right_stats, other, local_sem.at[4]).start()
+
+        @pl.when(half == 1)
+        def _():
+            pltpu.make_async_copy(right_stats, stat.at[rows_of(half)], local_sem.at[3]).start()
+            pltpu.make_async_copy(left_stats, other, local_sem.at[4]).start()
+        pair_own.start()
+        pair_right.start()
+        pair_left.start()
+
+        @pl.when(half == 0)
+        def _():
+            pair_stat(right_stats).start()
+
+        @pl.when(half == 1)
+        def _():
+            pair_stat(left_stats).start()
 
     def in_copy(to, sender):
         return remote(
@@ -175,14 +186,6 @@
         )
 
     gather_rows(lambda to: in_copy(to, chip))
-
-    @pl.when(half == 0)
-    def _():
-        pair_stat(right_stats).start()
-
-    @pl.when(half == 1)
-    def _():
-        pair_stat(left_stats).start()
 
     def pass_on(sender):
         slot = block.at[2 * sender + half]
@@ -213,11 +216,11 @@
 
     whole = block[...].reshape(size, size)
     mixed[...] = product(whole, right_whole[...]).astype(bf16)
-    cols[...] = (
-        product(left_some[...].reshape(half_rows, size), mixed[...])
-        .astype(bf16)
-        .reshape(cols.shape)
-    )
+
+    def update_rows(first, count):
+        part = left_some[pl.ds(first, count)].reshape(count * slab_rows, size)
+        part = product(part, mixed[...]).astype(bf16)
+        cols[pl.ds(first, count)] = part.reshape(count, slab_rows, size)
 
     def out_copy(to, sender):
         return remote(
@@ -240,7 +243,11 @@
             out_copy(turns[place], chip).wait_send()
 
     turns = sorted(range(chips), key=functools.partial(begins, chips))
-    for place in range(OUT_FLIGHT):
+    update_rows(0, per_half)
+    for place in range(min(OUT_FLIGHT, per_half)):
+        out_step(place)
+    update_rows(per_half, per_half)
+    for place in range(min(OUT_FLIGHT, per_half), OUT_FLIGHT):
         out_step(place)
     places = iter(range(OUT_FLIGHT, chips + OUT_FLIGHT))
 
@@ -312,9 +319,6 @@
     def _():
         fresh_left[...] = taken[...]
 
-    keep.wait()
-    for offset in near:
-        out_copy(peer(offset), peer(offset)).wait_recv()
     for offset in near:
         pass_on(peer(offset)).wait_send()
     gather_rest(lambda to: in_copy(to, chip))
@@ -323,6 +327,9 @@
     pair_left.wait_send()
     pair_stat(left_stats).wait_send()
     give.wait_send()
+    keep.wait()
+    for offset in near:
+        out_copy(peer(offset), peer(offset)).wait_recv()
 
 
 def final_kernel(

time: 44.3 us -> 43.9 us (level)
  the two profiles are of different devices: /device:TPU:93 before, /device:TPU:141 now
where the time goes in v4:
time: 43.9 us; the launch traced here: 43.8 us
  Pallas kernels  43.1 us (98%)
  between operations  0.67 us (2%)
    pallas_call x1, Pallas kernels, body(): pl.pallas_call(step_kernel, out_shape=(shaped((slab_rows, width), bf16),...  41.6 us
    pallas_call x1, Pallas kernels, body(): pl.pallas_call(final_kernel, out_shape=(shaped((slab_rows, width), bf16),...  1.51 us

profile of v4, /device:TPU:141, one launch (start us, length us, event | category | flops | bytes accessed | tf_op | source)
XLA Modules:
  0.0 43.8 jit_solution(16165946906919723268)
XLA Ops:
  0.6 0.0 copy-start
  0.6 0.0 copy-start.1
  0.7 41.6 %exchange.1 = (bf16[16,8192]{1,0:T(8,128)(2,1)S(1)}, f32[256,512]{1,0:T(8,128)S(1)}, f32[256,512]{1,0:T(8,128)S(1)}, bf16[256,512]{1,0:T(8,128)(2,1)S(1)}, bf16[256,512]{1,0:T(8,128)(2,1)S(1)}) custom-call(bf16[16,8192]{1,0:T(8,128)(2,1)} %grad.1, f32[256,512]{1,0:T(8,128)} %bitcast.13, f32[256,512]{1,0:T(8,128)} %bitcast.14, ...), custom_call_target="tpu_custom_call" | custom-call | tf_op jit(solution)/shard_map/exchange/pallas_call | solution.py:382
  42.2 0.0 copy-done
  42.2 0.0 copy-done.1
  42.2 1.5 %place.1 = (bf16[16,8192]{1,0:T(8,128)(2,1)}, f32[256,512]{1,0:T(8,128)}, f32[256,512]{1,0:T(8,128)}, bf16[256,512]{1,0:T(8,128)(2,1)}, bf16[256,512]{1,0:T(8,128)(2,1)}) custom-call(s32[1,4]{1,0:T(1,128)} %refresh.1, bf16[16,8192]{1,0:T(8,128)(2,1)S(1)} %get-tuple-element.15.update, f32[256,512]{1,0:T(8,128)S(1)} %get-tuple-element.16.new_left, ...), custom_call_target="tpu_custom_call" | custom-call | tf_op jit(solution)/shard_map/place/pallas_call | solution.py:413
Async XLA Ops:
  0.6 41.6 %copy-start = (bf16[1,256,512]{2,1,0:T(8,128)(2,1)S(1)}, bf16[1,256,512]{2,1,0:T(8,128)(2,1)}, u32[]{:S(2)}) copy-start(bf16[1,256,512]{2,1,0:T(8,128)(2,1)} %param.9) | copy-start | bytes 786436
  0.6 41.6 %copy-start.1 = (bf16[1,256,512]{2,1,0:T(8,128)(2,1)S(1)}, bf16[1,256,512]{2,1,0:T(8,128)(2,1)}, u32[]{:S(2)}) copy-start(bf16[1,256,512]{2,1,0:T(8,128)(2,1)} %param.10) | copy-start | bytes 786436
